TPU v7x, 768 devices: a whole 4x8x12 slice. The times are simulated.
768 devices in a mesh: dp: 12 (over z), expert: 64 (over x, y, core).
Axes of the slice: x: 4, y: 8, z: 12, core: 2. Of those that a mesh axis runs over, the one named last changes fastest.
Arguments:
- cotangent: bfloat16 [98304, 7168], P(('dp', 'expert')), may hold values from -6 to 6
- logits: float32 [98304, 8], P(('dp', 'expert')), may hold values from -8 to 8
- group_pick: int32 [98304, 8], P(('dp', 'expert')), may hold values from 0 to 7, as said below
- member_pick: int32 [98304, 8], P(('dp', 'expert')), may hold values from 0 to 31, as said below
- saved_gate: bfloat16 [1536, 8192], P('dp', 'expert'), may hold values from -6 to 6
- saved_up: bfloat16 [1536, 8192], P('dp', 'expert'), may hold values from -6 to 6
- gate_weight: bfloat16 [7168, 8192], P(None, 'expert'), may hold values from -0.0625 to 0.0625
- up_weight: bfloat16 [7168, 8192], P(None, 'expert'), may hold values from -0.0625 to 0.0625
- down_weight: bfloat16 [8192, 7168], P('expert'), may hold values from -0.125 to 0.125
Outputs:
- token_grad: bfloat16 [98304, 7168], P(('dp', 'expert'))
- logit_grad: float32 [98304, 8], P(('dp', 'expert'))
- down_grad: bfloat16 [8192, 7168], P('expert')
Inputs may be any that keep to these rules, and one draw needn't show every extreme that they name: Route k of token t goes to expert 32 * group_pick[t, k] + member_pick[t, k]; a token's 8 experts are distinct. Among the 128 tokens of one device no window expert is named more than 2 times, and one window expert is named exactly 2 times by the tokens of every device. `member_pick`: see group_pick.
All inputs are finite; a program needn't handle non-finite values.
Results may differ from a plain program's by a relative error of at most 0.02.
Values may be sent and summed in bfloat16 or wider, within the bound.
A program may use at most 64 MiB of HBM per device.

v0:
```python
import jax
import jax.numpy as jnp
from jax import lax
from jax.sharding import PartitionSpec as P

EXPERTS = 4
CAP = 2
GROUP_SIZE = 32
STRIDE = 64


route_scale = 2.5
highest = lax.Precision.HIGHEST


def rounded(values):
    return lax.optimization_barrier(values.astype(jnp.bfloat16)).astype(jnp.float32)


def body(
    cotangent,
    logits,
    group_pick,
    member_pick,
    saved_gate,
    saved_up,
    gate_weight,
    up_weight,
    down_weight,
):
    expert_ways = lax.axis_size("expert")
    hidden_blocks = expert_ways // EXPERTS
    token_count = cotangent.shape[0]
    width = cotangent.shape[1]
    chosen = group_pick * GROUP_SIZE + member_pick
    window_ids = jnp.arange(EXPERTS, dtype=jnp.int32) * STRIDE
    route_hits = (chosen[:, :, None] == window_ids[None, None, :]).astype(jnp.float32)
    in_window = jnp.sum(route_hits, axis=1)
    earlier = jnp.cumsum(in_window, axis=0) - in_window
    slot_numbers = jnp.arange(CAP, dtype=jnp.float32)
    slot_map = in_window.T[:, None, :] * (
        earlier.T[:, None, :] == slot_numbers[None, :, None]
    ).astype(jnp.float32)
    slot_flat = slot_map.reshape(EXPERTS * CAP, token_count)
    slot_narrow = slot_flat.astype(jnp.bfloat16)
    affinity = jax.nn.sigmoid(logits)
    affinity_sum = jnp.sum(affinity, axis=1, keepdims=True)
    gate_value = (route_scale * affinity / affinity_sum).astype(jnp.bfloat16)
    gate_wide = lax.optimization_barrier(gate_value).astype(jnp.float32)
    window_gate = jnp.einsum("tke,tk->te", route_hits, gate_wide, precision=highest)
    slot_gate = jnp.einsum("ect,te->ec", slot_map, window_gate, precision=highest)
    slot_grads = (
        jnp.dot(slot_narrow, cotangent, preferred_element_type=jnp.float32)
        .astype(jnp.bfloat16)
        .reshape(EXPERTS, CAP, width)
    )
    gate_pre = saved_gate.astype(jnp.float32).reshape(expert_ways, CAP, -1)
    up_pre = saved_up.astype(jnp.float32).reshape(expert_ways, CAP, -1)
    sigmoid_gate = jax.nn.sigmoid(gate_pre)
    activated = gate_pre * sigmoid_gate
    hidden = (activated * up_pre).astype(jnp.bfloat16)
    slice_out = jnp.einsum(
        "scf,fd->scd", hidden, down_weight, preferred_element_type=jnp.float32
    ).astype(jnp.bfloat16)
    outputs_back = lax.all_to_all(slice_out, "expert", split_axis=0, concat_axis=0, tiled=True)
    weighted_local = (slot_gate[:, :, None] * slot_grads.astype(jnp.float32)).astype(jnp.bfloat16)
    target = (EXPERTS, hidden_blocks) + weighted_local.shape[1:]
    weighted = lax.all_to_all(
        jnp.broadcast_to(weighted_local[:, None], target).reshape(
            (expert_ways,) + weighted_local.shape[1:]
        ),
        "expert",
        split_axis=0,
        concat_axis=0,
        tiled=True,
    )
    grad_hidden = jnp.einsum(
        "scd,fd->scf", weighted, down_weight, preferred_element_type=jnp.float32
    )
    grad_gate = (
        grad_hidden * up_pre * sigmoid_gate * (1.0 + gate_pre * (1.0 - sigmoid_gate))
    ).astype(jnp.bfloat16)
    grad_up = (grad_hidden * activated).astype(jnp.bfloat16)
    grad_rows = jnp.einsum(
        "scf,df->scd", grad_gate, gate_weight, preferred_element_type=jnp.float32
    )
    grad_rows = grad_rows + jnp.einsum(
        "scf,df->scd", grad_up, up_weight, preferred_element_type=jnp.float32
    )
    down_term = jnp.einsum("scf,scd->fd", hidden, weighted, preferred_element_type=jnp.float32)
    grad_rows, down_term = (grad_rows.astype(jnp.bfloat16), down_term)
    returned = lax.all_to_all(grad_rows, "expert", split_axis=0, concat_axis=0, tiled=True)
    router_dots = jnp.einsum(
        "wscd,wcd->wsc",
        outputs_back.reshape(EXPERTS, hidden_blocks, CAP, width),
        slot_grads,
        preferred_element_type=jnp.float32,
    )
    router_parts = rounded(router_dots)
    grad_slot = jnp.sum(
        returned.astype(jnp.float32).reshape(EXPERTS, hidden_blocks, CAP, width), axis=1
    ).reshape(EXPERTS * CAP, width)
    token_grad = jnp.dot(slot_flat.T, grad_slot, precision=highest).astype(jnp.bfloat16)
    router_slot = jnp.sum(router_parts, axis=1)
    window_grad = jnp.einsum("ect,ec->te", slot_map, router_slot, precision=highest)
    route_grad = jnp.einsum("tke,te->tk", route_hits, window_grad, precision=highest)
    spread_mean = jnp.sum(route_grad * affinity, axis=1, keepdims=True) / affinity_sum
    logit_grad = (
        affinity * (1.0 - affinity) * route_scale / affinity_sum * (route_grad - spread_mean)
    )
    down_grad = lax.psum(down_term.astype(jnp.bfloat16), "dp")
    return (token_grad, logit_grad, down_grad)


def solution(mesh):
    placed = (
        P(("dp", "expert"), None),
        P(("dp", "expert"), None),
        P(("dp", "expert"), None),
        P(("dp", "expert"), None),
        P("dp", "expert"),
        P("dp", "expert"),
        P(None, "expert"),
        P(None, "expert"),
        P("expert", None),
    )
    return jax.shard_map(
        body,
        mesh=mesh,
        in_specs=placed,
        out_specs=(P(("dp", "expert"), None), P(("dp", "expert"), None), P("expert", None)),
        check_vma=False,
    )
```

profile of v0, /device:TPU:6, one launch (start us, length us, event | category | flops | bytes accessed | tf_op | source)
XLA Modules:
  0.0 267.7 jit_solution(15251920707392845820)
XLA Ops:
  7.2 0.0 copy-start
  7.2 0.8 fusion.41
  8.0 0.7 divide_convert_fusion
  8.8 0.1 eq.45
  8.8 0.7 multiply_add_fusion
  9.6 0.1 fusion.16
  9.6 0.1 copy.38
  9.8 0.1 copy.41
  9.8 0.2 reduce_window_sum.13
  10.0 0.1 copy.40
  10.1 0.2 fusion.22
  10.3 1.9 convolution_convert_fusion.1
  12.2 0.1 reshape.60
  12.2 0.2 multiply_convert_fusion
  12.4 2.2 broadcast_in_dim.2
  14.6 14.8 %all-to-all-start = ((bf16[64,2,7168]{2,1,0:T(2,128)(2,1)}), bf16[64,2,7168]{2,1,0:T(2,128)(2,1)}, u32[]{:S(2)}, u32[]{:S(2)}) async-start(bf16[64,2,7168]{2,1,0:T(2,128)(2,1)} %bitcast.65), calls=%async_computation | async-start | bytes 3670016 | tf_op jit(solution)/shard_map/all_to_all | solution.py:68
  29.4 0.0 copy-done.4
  29.5 0.0 copy-done.5
  29.5 0.0 copy-done
  29.5 0.6 convolution_convert_fusion
  30.2 3.1 %copy.49 = bf16[64,2,7168]{2,1,0:T(2,128)(2,1)} copy(bf16[64,2,7168]{2,0,1:T(8,128)(2,1)S(1)} %convolution_convert_fusion) | data formatting | bytes 3670016 | tf_op jit(solution)/shard_map/convert_element_type | solution.py:64
  33.3 39.2 %all-to-all-done = bf16[64,2,7168]{2,1,0:T(2,128)(2,1)} async-done(((bf16[64,2,7168]{2,1,0:T(2,128)(2,1)}), bf16[64,2,7168]{2,1,0:T(2,128)(2,1)}, u32[]{:S(2)}, u32[]{:S(2)}) %all-to-all-start) | async-done | bytes 1835040 | tf_op jit(solution)/shard_map/all_to_all | solution.py:68
  72.5 8.6 %all-to-all-start.2 = ((bf16[64,2,7168]{2,1,0:T(2,128)(2,1)}), bf16[64,2,7168]{2,1,0:T(2,128)(2,1)}, u32[]{:S(2)}, u32[]{:S(2)}) async-start(bf16[64,2,7168]{2,1,0:T(2,128)(2,1)} %copy.49), calls=%async_computation.2 | async-start | bytes 3670016 | tf_op jit(solution)/shard_map/all_to_all | solution.py:65
  81.0 0.0 copy-start.2
  81.0 2.3 fusion.7
  83.3 0.0 copy-start.1
  83.3 0.6 fusion.4
  84.0 0.8 copy-done.1
  84.8 0.6 fusion
  85.5 3.1 %copy.47 = bf16[64,2,7168]{2,1,0:T(2,128)(2,1)} copy(bf16[64,2,7168]{2,0,1:T(8,128)(2,1)S(1)} %fusion) | data formatting | bytes 3670016 | tf_op jit(solution)/shard_map/convert_element_type | solution.py:91
  88.6 35.5 %all-to-all-done.2 = bf16[64,2,7168]{2,1,0:T(2,128)(2,1)} async-done(((bf16[64,2,7168]{2,1,0:T(2,128)(2,1)}), bf16[64,2,7168]{2,1,0:T(2,128)(2,1)}, u32[]{:S(2)}, u32[]{:S(2)}) %all-to-all-start.2) | async-done | bytes 1835040 | tf_op jit(solution)/shard_map/all_to_all | solution.py:65
  124.1 8.6 %all-to-all-start.1 = ((bf16[64,2,7168]{2,1,0:T(2,128)(2,1)}), bf16[64,2,7168]{2,1,0:T(2,128)(2,1)}, u32[]{:S(2)}, u32[]{:S(2)}) async-start(bf16[64,2,7168]{2,1,0:T(2,128)(2,1)} %copy.47), calls=%async_computation.1 | async-start | bytes 3670016 | tf_op jit(solution)/shard_map/all_to_all | solution.py:92
  132.6 0.2 all-reduce.2.cloned.1.call-start
  132.8 3.4 %fusion.2 = bf16[128,7168]{1,0:T(8,128)(2,1)} fusion(bf16[64,2,7168]{2,1,0:T(2,128)(2,1)} %all-to-all-done, f32[64,2,128]{2,1,0:T(2,128)S(1)} %convert.14, f32[64,2,128]{2,1,0:T(2,128)S(1)} %convert.13), kind=kOutput, calls=%fused_computation.5 | convolution fusion | flops 235896832 | bytes 3801088 | tf_op jit(solution)/shard_map/scf,scd->fd/dot_general | solution.py:90
  136.3 0.0 all-reduce.2.cloned.1.call-update
  136.3 0.0 copy-start.3
  136.3 0.1 reshape.91
  136.4 2.2 fusion.9
  138.7 0.1 convert_reduce_fusion.1
  138.7 0.1 copy.61
  138.8 0.2 fusion.21
  139.0 0.1 select_reduce_fusion
  139.1 0.6 fusion.20
  139.8 35.9 %all-to-all-done.1 = bf16[64,2,7168]{2,1,0:T(2,128)(2,1)} async-done(((bf16[64,2,7168]{2,1,0:T(2,128)(2,1)}), bf16[64,2,7168]{2,1,0:T(2,128)(2,1)}, u32[]{:S(2)}, u32[]{:S(2)}) %all-to-all-start.1) | async-done | bytes 1835040 | tf_op jit(solution)/shard_map/all_to_all | solution.py:92
  175.7 3.1 %convert_reduce_fusion = f32[4,2,7168]{2,1,0:T(2,128)S(1)} fusion(bf16[64,2,7168]{2,1,0:T(2,128)(2,1)} %all-to-all-done.1), kind=kLoop, calls=%fused_computation.8 | loop fusion | flops 1777664 | bytes 2064384 | tf_op jit(solution)/shard_map/reduce_sum | solution.py:100
  178.8 4.3 %fusion.1 = bf16[128,7168]{1,0:T(8,128)(2,1)} fusion(f32[4,2,7168]{2,1,0:T(2,128)S(1)} %convert_reduce_fusion, f32[4,128]{1,0:T(4,128)S(1)} %copy.41, f32[4,128]{1,0:T(4,128)S(1)} %copy.40), kind=kOutput, calls=%fused_computation.4 | convolution fusion | flops 88999936 | bytes 2068480 | tf_op jit(solution)/shard_map/dot_general | solution.py:103
  183.1 74.8 %all-reduce.2.cloned.1.call-done = bf16[128,7168]{1,0:T(8,128)(2,1)} async-done(((bf16[128,7168]{1,0:T(8,128)(2,1)}), bf16[128,7168]{1,0:T(8,128)(2,1)}) %all-reduce.2.cloned.1.call-update) | async-done | bytes 1835024 | tf_op jit(solution)/shard_map/psum | solution.py:111
  258.0 2.8 %copy.99 = bf16[128,7168]{1,0:T(8,128)(2,1)} copy(bf16[128,7168]{1,0:T(8,128)(2,1)} %all-reduce.2.cloned.1.call-done) | data formatting | bytes 3670016
  (15 shorter events, 0.1 us)
Async XLA Ops:
  7.2 22.3 %copy-start = (bf16[128,7168]{1,0:T(8,128)(2,1)S(1)}, bf16[128,7168]{1,0:T(8,128)(2,1)}, u32[]{:S(2)}) copy-start(bf16[128,7168]{1,0:T(8,128)(2,1)} %param.17) | copy-start | bytes 5505028
  14.6 14.8 %copy-start.4 = (bf16[128,128]{1,0:T(8,128)(2,1)S(1)}, bf16[128,128]{1,0:T(8,128)(2,1)}, u32[]{:S(2)}) copy-start(bf16[128,128]{1,0:T(8,128)(2,1)} %param.13) | copy-start | bytes 98308
  14.6 14.9 %copy-start.5 = (bf16[128,128]{1,0:T(8,128)(2,1)S(1)}, bf16[128,128]{1,0:T(8,128)(2,1)}, u32[]{:S(2)}) copy-start(bf16[128,128]{1,0:T(8,128)(2,1)} %param.14) | copy-start | bytes 98308
  14.6 57.9 %all-to-all-start = ((bf16[64,2,7168]{2,1,0:T(2,128)(2,1)}), bf16[64,2,7168]{2,1,0:T(2,128)(2,1)}, u32[]{:S(2)}, u32[]{:S(2)}) async-start(bf16[64,2,7168]{2,1,0:T(2,128)(2,1)} %bitcast.65), calls=%async_computation | async-start | bytes 3670016 | tf_op jit(solution)/shard_map/all_to_all | solution.py:68
  72.5 51.6 %all-to-all-start.2 = ((bf16[64,2,7168]{2,1,0:T(2,128)(2,1)}), bf16[64,2,7168]{2,1,0:T(2,128)(2,1)}, u32[]{:S(2)}, u32[]{:S(2)}) async-start(bf16[64,2,7168]{2,1,0:T(2,128)(2,1)} %copy.49), calls=%async_computation.2 | async-start | bytes 3670016 | tf_op jit(solution)/shard_map/all_to_all | solution.py:65
  81.0 2.3 copy-start.2
  83.3 1.5 copy-start.1
  124.1 51.6 %all-to-all-start.1 = ((bf16[64,2,7168]{2,1,0:T(2,128)(2,1)}), bf16[64,2,7168]{2,1,0:T(2,128)(2,1)}, u32[]{:S(2)}, u32[]{:S(2)}) async-start(bf16[64,2,7168]{2,1,0:T(2,128)(2,1)} %copy.47), calls=%async_computation.1 | async-start | bytes 3670016 | tf_op jit(solution)/shard_map/all_to_all | solution.py:92
  132.6 125.3 %all-reduce.2.cloned.1.call-start = ((), (), s32[]{:S(2)}) async-start(), calls=%async_computation.3 | async-start | bytes 3670016 | tf_op jit(solution)/shard_map/psum | solution.py:111
  136.3 2.8 %copy-start.3 = (f32[128,8]{0,1:T(8,128)S(1)}, f32[128,8]{0,1:T(8,128)}, u32[]{:S(2)}) copy-start(f32[128,8]{0,1:T(8,128)} %param.10) | copy-start | bytes 12292
Sparse Core Ops, SparseCore 0:
  136.4 121.4 all-reduce.1
where the time goes:
time: 268 us
  waiting for transfers between devices  185 us (69%)
  starting transfers between devices  32.2 us (12%)
  matrix products  16.4 us (6%)
  between operations  14.2 us (5%)
  local copies, waits for them, and re-layouts  12.7 us (5%)
  other arithmetic  6.72 us (3%)
    psum x1, waiting for transfers between devices, body(): down_grad = lax.psum(down_term.astype(jnp.bfloat16), 'dp')  74.8 us
    all_to_all x1, waiting for transfers between devices, body(): lax.all_to_all(jnp.broadcast_to(weighted_local[:, None], target).reshape(...  39.2 us
    all_to_all x1, waiting for transfers between devices, body(): lax.all_to_all(grad_rows, 'expert', split_axis=0, concat_axis=0, tiled=True)  35.9 us
    all_to_all x1, waiting for transfers between devices, body(): lax.all_to_all(slice_out, 'expert', split_axis=0, concat_axis=0, tiled=True)  35.5 us
    all_to_all x1, starting transfers between devices, body(): lax.all_to_all(jnp.broadcast_to(weighted_local[:, None], target).reshape(...  14.8 us
    all_to_all x1, starting transfers between devices, body(): lax.all_to_all(slice_out, 'expert', split_axis=0, concat_axis=0, tiled=True)  8.56 us
    all_to_all x1, starting transfers between devices, body(): lax.all_to_all(grad_rows, 'expert', split_axis=0, concat_axis=0, tiled=True)  8.56 us
  transfers between devices with their start and end apart: 4, of which 4 were waited for; matrix products, arithmetic and copies ran while one was open for 9% of the time, Pallas kernels for 0%

commit v1 on v0

v1 whole, which is shorter than its diff:
```python
import functools

import jax
import jax.numpy as jnp
from jax import lax
from jax.experimental import pallas as pl
from jax.experimental.pallas import tpu as pltpu
from jax.sharding import PartitionSpec as P

EXPERTS = 4
CAP = 2
GROUP_SIZE = 32
STRIDE = 64
route_scale = 2.5
MESH = pl.DeviceIdType.MESH
bf16 = jnp.bfloat16
f32 = jnp.float32

NX = EXPERTS
NY = 8
NZ = 12
SPAN = 640


def iota(shape, dim):
    return lax.broadcasted_iota(jnp.int32, shape, dim)


def one_hot(mask):
    return jnp.where(mask, 1.0, 0.0).astype(bf16)


def mm(a, b, ca=1, cb=0):
    return lax.dot_general(a, b, (((ca,), (cb,)), ((), ())), preferred_element_type=f32)


def split(v):
    hi = v.astype(bf16)
    rest = v - hi.astype(f32)
    mid = rest.astype(bf16)
    low = (rest - mid.astype(f32)).astype(bf16)
    return hi, mid, low


def routing(logits, group, member):
    chosen = group * GROUP_SIZE + member
    affinity = jax.nn.sigmoid(logits)
    affinity_sum = jnp.sum(affinity, axis=0, keepdims=True)
    gate = (route_scale * affinity / affinity_sum).astype(bf16).astype(f32)
    row = iota(chosen.shape, 0)
    hits = [chosen == w * STRIDE for w in range(EXPERTS)]
    member8 = jnp.zeros(chosen.shape, f32)
    gate8 = jnp.zeros(chosen.shape, f32)
    for w in range(EXPERTS):
        in_window = jnp.sum(jnp.where(hits[w], 1.0, 0.0), axis=0, keepdims=True)
        window_gate = jnp.sum(jnp.where(hits[w], gate, 0.0), axis=0, keepdims=True)
        mine = (row // CAP) == w
        member8 = jnp.where(mine, in_window, member8)
        gate8 = jnp.where(mine, window_gate, gate8)
    tokens = chosen.shape[1]
    before = one_hot(iota((tokens, tokens), 0) < iota((tokens, tokens), 1))
    earlier = mm(member8.astype(bf16), before)
    slot8 = jnp.where(earlier == (row % CAP).astype(f32), member8, 0.0)
    return affinity, affinity_sum, hits, slot8, gate8


def expand_rows(rows):
    i = iota((rows, EXPERTS * CAP), 0)
    j = iota((rows, EXPERTS * CAP), 1)
    per = rows // EXPERTS
    return one_hot((i // per) * CAP + i % CAP == j)


def main_kernel(
    logits_ref, group_ref, member_ref, sg_ref, su_ref, cot_hbm, gate_hbm, up_hbm, down_hbm,
    yr, dg,
    cotv, downv, guv, xs, xr, av, w2, hv, gp, upv, own, qs, qr, p0, p1, sm0, sm1, rm0, rm1, ys,
    load_sem,
    xs_s, xs_r, za_s, za_r, a_s, a_r, as_s, as_r, b_s, b_r, bs_s, bs_r, h_s, h_r, o_s, o_r,
    q_s, q_r, m_s, m_r, y_s, y_r, loc,
):
    e = lax.axis_index("expert")
    z = lax.axis_index("dp")
    x = e // (2 * NY)
    y = (e // 2) % NY
    c = e % 2
    other = 1 - c
    half = cotv.shape[0] // 2
    seg = cotv.shape[2]
    subw = seg * 2
    pending = []

    def at(zz, xx, yy, cc):
        return (zz, (xx * NY + yy) * 2 + cc)

    def send(src, dst, ssem, rsem, dev):
        copy = pltpu.make_async_remote_copy(
            src_ref=src, dst_ref=dst, send_sem=ssem, recv_sem=rsem, device_id=dev, device_id_type=MESH
        )
        copy.start()
        pending.append(copy)

    def arrived(dst, rsem):
        pltpu.make_async_remote_copy(
            src_ref=dst, dst_ref=dst, send_sem=rsem, recv_sem=rsem,
            device_id=at(z, x, y, other), device_id_type=MESH,
        ).wait_recv()

    loads = []

    def load(src, dst, k):
        copy = pltpu.make_async_copy(src, dst, load_sem.at[k])
        copy.start()
        loads.append(copy)

    for j in range(8):
        load(cot_hbm.at[:, pl.ds(j * seg, seg)], cotv.at[j], j)
    for j in range(4):
        load(down_hbm.at[:, pl.ds(j * subw, subw)], downv.at[j], 8 + j)
    for j in range(8):
        load(gate_hbm.at[pl.ds(j * seg, seg), :], guv.at[j, :, pl.ds(0, 128)], 12 + j)
        load(up_hbm.at[pl.ds(j * seg, seg), :], guv.at[j, :, pl.ds(128, 128)], 20 + j)

    barrier = pltpu.get_barrier_semaphore()
    greeted = 0

    def greet(dev):
        pl.semaphore_signal(barrier, inc=1, device_id=dev, device_id_type=MESH)

    for dz in range(NZ):
        for dc in range(2):
            if dz or dc:
                greet(at((z + dz) % NZ, x, y, (c + dc) % 2))
                greeted += 1
    for dx in range(1, NX):
        for dc in range(2):
            greet(at(z, (x + dx) % NX, y, (c + dc) % 2))
            greeted += 1
    for dy in (1, NY - 1):
        greet(at(z, x, (y + dy) % NY, c))
        greeted += 1

    def own_hidden():
        i = iota((128, 128), 0)
        k = iota((128, 128), 1)
        perm = one_hot(k == ((i // 4) % NX) * (4 * NY) + (i // (4 * NX)) * 4 + i % 4)
        gp[...] = mm(perm, sg_ref[...])
        upv[...] = mm(perm, su_ref[...])
        gate_pre = gp[...]
        hidden = (gate_pre * jax.nn.sigmoid(gate_pre) * upv[...]).astype(bf16)
        zz = z // 2
        hv[z % 2, zz // 3, :, zz % 3] = hidden.reshape(NY, 16, 128)

    own_hidden()

    affinity, affinity_sum, hits, slot8, gate8 = routing(logits_ref[...], group_ref[...], member_ref[...])
    rows64 = mm(expand_rows(64), (slot8 * gate8).astype(bf16))
    rowseg = (iota((64, 128), 0) // CAP) % 8
    spread = jnp.concatenate(
        [jnp.where(rowseg == j, rows64, 0.0).astype(bf16) for j in range(8)], axis=1
    )
    for j in range(8):
        loads[j].wait()
    gated = mm(spread, cotv[...].reshape(8 * 128, seg))
    xs[...] = gated.reshape(NX, 2, 8, seg)

    pl.semaphore_wait(barrier, greeted)

    h_steps = [(0, t) for t in range(NZ // 2)] + [(1, t) for t in range(NZ // 2 - 1)]

    def hchunk(zz):
        return hv.at[zz % 2, (zz // 2) // 3, :, (zz // 2) % 3]

    def h_send(d, t):
        s = 1 if d == 0 else -1
        ref = hchunk((z - s * t + NZ) % NZ)
        k = d * (NZ // 2) + t
        send(ref, ref, h_s.at[k], h_r.at[k], at((z + s + NZ) % NZ, x, y, c))

    def h_recv(d, t):
        s = 1 if d == 0 else -1
        arrived(hchunk((z - s * (t + 1) + NZ) % NZ), h_r.at[d * (NZ // 2) + t])
        if (d, t + 1) in h_steps:
            h_send(d, t + 1)

    keep = pltpu.make_async_copy(xs.at[x, c], xr.at[x, c], xs_r.at[x * 2 + c])
    for dx in range(NX):
        for dc in range(2):
            if dx == 0 and dc == 0:
                keep.start()
                continue
            xx, cc = (x + dx) % NX, (c + dc) % 2
            send(xs.at[xx, cc], xr.at[x, c], xs_s.at[dx * 2 + dc], xs_r.at[x * 2 + c], at(z, xx, y, cc))
    h_send(0, 0)
    h_send(1, 0)
    for xx in range(NX):
        for cc in range(2):
            arrived(xr.at[xx, cc], xs_r.at[xx * 2 + cc])
    i16 = iota((16, 64), 0)
    k16 = iota((16, 64), 1)
    got = xr[...].reshape(64, seg).astype(bf16)
    for s in range(4):
        pick = one_hot(((k16 // 8) * CAP + k16 % CAP == i16) & ((k16 // CAP) % 4 == s))
        av[c, s // 2, y, :, pl.ds((s % 2) * seg, seg)] = mm(pick, got).astype(bf16)

    def ring(buf, ssem, rsem, sib_s, sib_r):
        steps = {(d, s): (NY // 2 if d == s else NY // 2 - 1) for d in range(2) for s in range(2)}

        def number(d, s, t):
            return (d * 2 + s) * (NY // 2) + t

        def put(d, s, t):
            g = 1 if d == 0 else -1
            ref = buf.at[c, s, (y - g * t + NY) % NY]
            k = number(d, s, t)
            send(ref, ref, ssem.at[k], rsem.at[k], at(z, x, (y + g + NY) % NY, c))

        def across(yy, s, k):
            ref = buf.at[c, s, yy]
            send(ref, ref, sib_s.at[k], sib_r.at[k], at(z, x, y, other))

        def first():
            for s in range(2):
                put(0, s, 0)
                put(1, s, 0)
            for s in range(2):
                across(y, s, 16 + s)

        def turn(t):
            for s in range(2):
                for d in range(2):
                    if t < steps[d, s]:
                        g = 1 if d == 0 else -1
                        yy = (y - g * (t + 1) + NY) % NY
                        k = number(d, s, t)
                        arrived(buf.at[c, s, yy], rsem.at[k])
                        if t + 1 < steps[d, s]:
                            put(d, s, t + 1)
                        across(yy, s, k)

        def last():
            for s in range(2):
                arrived(buf.at[other, s, y], sib_r.at[16 + s])
                for d in range(2):
                    g = 1 if d == 0 else -1
                    for t in range(steps[d, s]):
                        yy = (y - g * (t + 1) + NY) % NY
                        arrived(buf.at[other, s, yy], sib_r.at[number(d, s, t)])

        return first, turn, last

    a_first, a_turn, a_last = ring(av, a_s, a_r, as_s, as_r)
    b_first, b_turn, b_last = ring(w2, b_s, b_r, bs_s, bs_r)
    a_first()

    def first_tile(k):
        return (14 * k) // 3

    zq = z // 2
    per_half = NZ // 2
    for k in range(per_half):
        zz = c * per_half + k
        start = first_tile(k) * 128
        src = av.at[c, start // subw, y, :, pl.ds(start % subw, SPAN)]
        dst = w2.at[z % 2, zq // 3, y, zq % 3]
        copy = pltpu.make_async_remote_copy(
            src_ref=src, dst_ref=dst, send_sem=za_s.at[k], recv_sem=za_r.at[zq],
            device_id=at(zz, x, y, z % 2), device_id_type=MESH,
        )
        here = pltpu.make_async_copy(src, dst, za_r.at[zq])
        remote = jnp.logical_or(zz != z, z % 2 != c)

        @pl.when(remote)
        def _(copy=copy):
            copy.start()

        @pl.when(jnp.logical_not(remote))
        def _(here=here):
            here.start()
        pending.append((copy, remote))
    for q in range(NZ // 2):
        arrived(w2.at[c, q // 3, y, q % 3], za_r.at[q])
    b_first()

    for t in range(NY // 2):
        a_turn(t)
        b_turn(t)
        for k in (t * 2, t * 2 + 1):
            for d in range(2):
                if (d, k) in h_steps:
                    h_recv(d, k)
    b_last()

    mine = mm(hv[...].reshape(-1, 128), w2[...].reshape(-1, SPAN), 0, 0).astype(bf16)
    own[...] = mine.reshape(2, 64, SPAN)
    keep_out = pltpu.make_async_copy(own, dg.at[z], loc.at[0])
    keep_out.start()
    o_steps = {(d, s): (NZ // 2 if d == s else NZ // 2 - 1) for d in range(2) for s in range(2)}

    def o_send(d, s, t):
        g = 1 if d == 0 else -1
        zz = (z - g * t + NZ) % NZ
        k = (d * 2 + s) * (NZ // 2) + t
        src = own.at[s] if t == 0 else dg.at[zz, s]
        send(src, dg.at[zz, s], o_s.at[k], o_r.at[k], at((z + g + NZ) % NZ, x, y, c))

    def o_turn(t):
        for s in range(2):
            for d in range(2):
                if t < o_steps[d, s]:
                    g = 1 if d == 0 else -1
                    k = (d * 2 + s) * (NZ // 2) + t
                    arrived(dg.at[(z - g * (t + 1) + NZ) % NZ, s], o_r.at[k])
                    if t + 1 < o_steps[d, s]:
                        o_send(d, s, t + 1)

    for s in range(2):
        o_send(0, s, 0)
        o_send(1, s, 0)

    a_last()
    for j in range(8, 28):
        loads[j].wait()
    grad_hidden = mm(av[0, 0].reshape(128, subw), downv[0], 1, 1)
    for j in range(1, 4):
        grad_hidden += mm(av[j // 2, j % 2].reshape(128, subw), downv[j], 1, 1)
    gate_pre = gp[...]
    up_pre = upv[...]
    sig = jax.nn.sigmoid(gate_pre)
    act = gate_pre * sig
    hidden = (act * up_pre).astype(bf16).astype(f32)
    p1[:, :, pl.ds(subw, 128)] = (hidden * grad_hidden).reshape(NY, 16, 128)
    grad_gate = (grad_hidden * up_pre * sig * (1.0 + gate_pre * (1.0 - sig))).astype(bf16)
    grad_up = (grad_hidden * act).astype(bf16)
    both = jnp.concatenate([grad_gate, grad_up], axis=1)
    for s in range(4):
        qs[s] = mm(both, guv[other * 4 + s], 1, 1).astype(bf16)
        send(qs.at[s], qr.at[s], q_s.at[s], q_r.at[s], at(z, x, y, other))
    for s in range(4):
        part = mm(both, guv[c * 4 + s], 1, 1)
        (p0, p1)[s // 2][:, :, pl.ds((s % 2) * seg, seg)] = part.reshape(NY, 16, seg)

    pp, sm, rm = (p0, p1), (sm0, sm1), (rm0, rm1)
    m_steps = {(d, s): (NY // 2 if d == s else NY // 2 - 1) for d in range(2) for s in range(2)}

    def m_number(d, t):
        return d * (NY // 2) + t

    def m_send(d, s, t):
        g = 1 if d == 0 else -1
        left = m_steps[d, s] - t
        value = pp[s][(y + g * left + NY) % NY]
        n = m_number(d, t)
        if t:
            value = value + rm[s][m_number(d, t - 1)].astype(f32)
        sm[s][n] = value.astype(bf16)
        send(sm[s].at[n], rm[s].at[n], m_s.at[s * 8 + n], m_r.at[s * 8 + n], at(z, x, (y + g + NY) % NY, c))

    for s in range(4):
        arrived(qr.at[s], q_r.at[s])
        ref = (p0, p1)[s // 2]
        cols = pl.ds((s % 2) * seg, seg)
        ref[:, :, cols] = ref[:, :, cols] + qr[s].astype(f32).reshape(NY, 16, seg)
        if s % 2:
            m_send(0, s // 2, 0)
            m_send(1, s // 2, 0)
    for t in range(NY // 2):
        for s in range(2):
            for d in range(2):
                if t < m_steps[d, s]:
                    n = m_number(d, t)
                    arrived(rm[s].at[n], m_r.at[s * 8 + n])
                    if t + 1 < m_steps[d, s]:
                        m_send(d, s, t + 1)
        o_turn(t)

    i64 = iota((64, 16), 0)
    k64 = iota((64, 16), 1)
    totals = []
    for s in range(2):
        total = pp[s][y]
        for d in range(2):
            total = total + rm[s][m_number(d, m_steps[d, s] - 1)].astype(f32)
        totals.append(total)
    out = jnp.zeros((64, seg), f32)
    source = (i64 // 8) * CAP + i64 % CAP
    for s in range(4):
        pick = one_hot((source == k64) & ((i64 // CAP) % 4 == s))
        for piece in split(totals[s // 2][:, (s % 2) * seg:(s % 2) * seg + seg]):
            out = out + mm(pick, piece)
    products = jnp.zeros((64, 128), f32)
    pick = one_hot((source == k64) & ((i64 // CAP) % 4 == 0))
    for piece in split(totals[1][:, subw:subw + 128]):
        products = products + mm(pick, piece)
    ys[:, :, :, pl.ds(0, seg)] = out.reshape(NX, 2, 8, seg)
    ys[:, :, :, pl.ds(seg, 128)] = products.reshape(NX, 2, 8, 128)
    keep = pltpu.make_async_copy(ys.at[x, c], yr.at[x, c], y_r.at[x * 2 + c])
    for dx in range(NX):
        for dc in range(2):
            if dx == 0 and dc == 0:
                keep.start()
                continue
            xx, cc = (x + dx) % NX, (c + dc) % 2
            send(ys.at[xx, cc], yr.at[x, c], y_s.at[dx * 2 + dc], y_r.at[x * 2 + c], at(z, xx, y, cc))
    for t in range(NY // 2, NZ // 2):
        o_turn(t)
    for xx in range(NX):
        for cc in range(2):
            arrived(yr.at[xx, cc], y_r.at[xx * 2 + cc])
    keep_out.wait()
    for item in pending:
        if isinstance(item, tuple):
            copy, cond = item

            @pl.when(cond)
            def _(copy=copy):
                copy.wait_send()
        else:
            item.wait_send()


def final_kernel(
    logits_ref, group_ref, member_ref, yr_ref, dg, token_out, logit_ref, down_out, stage, sems
):
    seg = stage.shape[2]
    per_half = NZ // 2
    copies = []
    for zz in range(NZ):
        k = zz % per_half
        start = (14 * k) // 3
        width = ((14 * (k + 1)) // 3 - start) * 128
        start = (zz // per_half) * 4 * seg + start * 128
        for s in range(2):
            copy = pltpu.make_async_copy(
                dg.at[zz, s, :, pl.ds(0, width)],
                down_out.at[pl.ds(s * 64, 64), pl.ds(start, width)],
                sems.at[8 + zz * 2 + s],
            )
            copy.start()
            copies.append(copy)
    affinity, affinity_sum, hits, slot8, gate8 = routing(logits_ref[...], group_ref[...], member_ref[...])
    grads = yr_ref[:, :, :, 0:seg].reshape(64, seg)
    pieces = jnp.concatenate(split(grads), axis=0)
    expand = expand_rows(64)
    place = mm(slot8.astype(bf16), expand, 0, 1)
    colseg = (iota((128, 64), 1) // CAP) % 8
    for j in range(8):
        chosen = jnp.where(colseg == j, place, 0.0).astype(bf16)
        stage[j] = mm(jnp.concatenate([chosen] * 3, axis=1), pieces).astype(bf16)
        copy = pltpu.make_async_copy(stage.at[j], token_out.at[:, pl.ds(j * seg, seg)], sems.at[j])
        copy.start()
        copies.append(copy)
    products = yr_ref[:, :, :, seg:seg + 128].reshape(64, 128)
    folded = jnp.zeros((8, 128), f32)
    for piece in split(products):
        folded = folded + mm(expand, piece, 0, 0)
    router = jnp.sum(folded, axis=1, keepdims=True)
    used = slot8 > 0.0
    routes = jnp.where(used, router / jnp.where(used, gate8, 1.0), 0.0)
    row = iota(slot8.shape, 0)
    route_grad = jnp.zeros(slot8.shape, f32)
    for w in range(EXPERTS):
        window_grad = jnp.sum(jnp.where((row // CAP) == w, routes, 0.0), axis=0, keepdims=True)
        route_grad = jnp.where(hits[w], window_grad, route_grad)
    mean = jnp.sum(route_grad * affinity, axis=0, keepdims=True) / affinity_sum
    logit_ref[...] = affinity * (1.0 - affinity) * route_scale / affinity_sum * (route_grad - mean)
    for copy in copies:
        copy.wait()


def body(cotangent, logits, group_pick, member_pick, saved_gate, saved_up, gate_weight, up_weight, down_weight):
    tokens, width = cotangent.shape
    seg = width // 8
    subw = 2 * seg
    vmem = pl.BlockSpec(memory_space=pltpu.VMEM)
    hbm = pl.BlockSpec(memory_space=pl.ANY)
    logits_t, group_t, member_t = logits.T, group_pick.T, member_pick.T
    dma = pltpu.SemaphoreType.DMA
    scratch = [
        pltpu.VMEM((8, tokens, seg), bf16),
        pltpu.VMEM((4, 128, subw), bf16),
        pltpu.VMEM((8, seg, 256), bf16),
        pltpu.VMEM((NX, 2, 8, seg), f32),
        pltpu.VMEM((NX, 2, 8, seg), f32),
        pltpu.VMEM((2, 2, NY, 16, subw), bf16),
        pltpu.VMEM((2, 2, NY, 3, 16, SPAN), bf16),
        pltpu.VMEM((2, 2, NY, 3, 16, 128), bf16),
        pltpu.VMEM((128, 128), f32),
        pltpu.VMEM((128, 128), f32),
        pltpu.VMEM((2, 64, SPAN), bf16),
        pltpu.VMEM((4, 128, seg), bf16),
        pltpu.VMEM((4, 128, seg), bf16),
        pltpu.VMEM((NY, 16, subw), f32),
        pltpu.VMEM((NY, 16, subw + 128), f32),
        pltpu.VMEM((8, 16, subw), bf16),
        pltpu.VMEM((8, 16, subw + 128), bf16),
        pltpu.VMEM((8, 16, subw), bf16),
        pltpu.VMEM((8, 16, subw + 128), bf16),
        pltpu.VMEM((NX, 2, 8, seg + 128), f32),
        dma((28,)),
        dma((8,)), dma((8,)),
        dma((6,)), dma((6,)),
        dma((16,)), dma((16,)), dma((18,)), dma((18,)),
        dma((16,)), dma((16,)), dma((18,)), dma((18,)),
        dma((12,)), dma((12,)),
        dma((24,)), dma((24,)),
        dma((4,)), dma((4,)),
        dma((16,)), dma((16,)),
        dma((8,)), dma((8,)),
        dma((1,)),
    ]
    yr, dg = pl.pallas_call(
        main_kernel,
        out_shape=(
            jax.ShapeDtypeStruct((NX, 2, 8, seg + 128), f32),
            jax.ShapeDtypeStruct((NZ, 2, 64, SPAN), bf16),
        ),
        in_specs=[vmem] * 5 + [hbm] * 4,
        out_specs=(hbm, hbm),
        scratch_shapes=scratch,
        compiler_params=pltpu.CompilerParams(
            collective_id=0, has_side_effects=True, vmem_limit_bytes=62 * 1024 * 1024
        ),
    )(logits_t, group_t, member_t, saved_gate, saved_up, cotangent, gate_weight, up_weight, down_weight)
    token_grad, logit_grad, down_grad = pl.pallas_call(
        final_kernel,
        out_shape=(
            jax.ShapeDtypeStruct((tokens, width), bf16),
            jax.ShapeDtypeStruct((8, tokens), f32),
            jax.ShapeDtypeStruct((128, width), bf16),
        ),
        in_specs=[vmem] * 4 + [hbm],
        out_specs=(hbm, vmem, hbm),
        scratch_shapes=[pltpu.VMEM((8, tokens, seg), bf16), dma((32,))],
        compiler_params=pltpu.CompilerParams(vmem_limit_bytes=62 * 1024 * 1024),
    )(logits_t, group_t, member_t, yr, dg)
    return token_grad, logit_grad.T, down_grad


def solution(mesh):
    placed = (
        P(("dp", "expert"), None),
        P(("dp", "expert"), None),
        P(("dp", "expert"), None),
        P(("dp", "expert"), None),
        P("dp", "expert"),
        P("dp", "expert"),
        P(None, "expert"),
        P(None, "expert"),
        P("expert", None),
    )
    return jax.shard_map(
        body,
        mesh=mesh,
        in_specs=placed,
        out_specs=(P(("dp", "expert"), None), P(("dp", "expert"), None), P("expert", None)),
        check_vma=False,
    )
```

time: 268 us -> 152 us (0.57)
  waiting for transfers between devices: 185 us -> 0 us
  Pallas kernels: 0 us -> 149 us
  starting transfers between devices: 32.2 us -> 0 us
  matrix products: 16.4 us -> 0 us
  between operations: 14.2 us -> 0.64 us
  local copies, waits for them, and re-layouts: 12.7 us -> 0 us
  other arithmetic: 6.72 us -> 0 us
    pallas_call x0 -> x2, Pallas kernels: none -> 149 us  [the longest x1 90.3 us: body(): pl.pallas_call(main_kernel, out_shape=(jax.ShapeDtypeStruct((NX, 2, 8, se...]
    all_to_all x3 -> x0, waiting for transfers between devices: 111 us -> none  [the longest x1 39.2 us: body(): lax.all_to_all(jnp.broadcast_to(weighted_local[:, None], target).reshape(...]
    psum x1 -> x0, waiting for transfers between devices: 74.8 us -> none  [body(): down_grad = lax.psum(down_term.astype(jnp.bfloat16), 'dp')]
    all_to_all x3 -> x0, starting transfers between devices: 31.9 us -> none  [the longest x1 14.8 us: body(): lax.all_to_all(jnp.broadcast_to(weighted_local[:, None], target).reshape(...]
    dot_general x10 -> x0, matrix products: 16.4 us -> none  [the longest x1 4.34 us: body(): jnp.dot(slot_flat.T, grad_slot, precision=highest).astype(jnp.bfloat16)]
    convert_element_type x2 -> x0, local copies, waits for them, and re-layouts: 6.23 us -> none  [the longest x1 3.12 us: body(): slice_out = jnp.einsum('scf,fd->scd', hidden, down_weight, preferred_elem...]
    reduce_sum x4 -> x0, other arithmetic: 4.08 us -> none  [the longest x1 3.12 us: body(): jnp.sum(returned.astype(jnp.float32).reshape(EXPERTS, hidden_blocks, CAP,...]
    unnamed x13 -> x0, local copies, waits for them, and re-layouts: 3.72 us -> none
  transfers between devices with their start and end apart: 4 -> 0, of which waited for: 4 -> 0; matrix products, arithmetic and copies ran while one was open for 9% -> 0% of each run, Pallas kernels for 0% -> 0%
where the time goes in v1:
time: 152 us; the launch traced here: 149 us
  Pallas kernels  149 us (98%)
    pallas_call x1, Pallas kernels, body(): pl.pallas_call(main_kernel, out_shape=(jax.ShapeDtypeStruct((NX, 2, 8, se...  90.3 us
    pallas_call x1, Pallas kernels, body(): pl.pallas_call(final_kernel, out_shape=(jax.ShapeDtypeStruct((tokens, wid...  58.6 us

profile of v1, /device:TPU:6, one launch (start us, length us, event | category | flops | bytes accessed | tf_op | source)
XLA Modules:
  0.0 149.5 jit_solution(9529230396085446637)
XLA Ops:
  0.6 90.3 %shard_map.112 = (f32[4,2,8,1024]{3,2,1,0:T(8,128)}, bf16[12,2,64,640]{3,2,1,0:T(8,128)(2,1)}) custom-call(f32[8,128]{1,0:T(8,128)} %bitcast.4, s32[8,128]{1,0:T(8,128)} %bitcast.6, s32[8,128]{1,0:T(8,128)} %bitcast.8, bf16[128,128]{1,0:T(8,128)(2,1)} %sg_ref.1, bf16[128,128]{1,0:T(8,128)(2,1)} %su_ref.1, bf16[128,7168]{1,0:T(8,128)(2,1)} %cot_hbm.1, ...), custom_call_target="tpu_custom_call" | custom-call | tf_op jit(solution)/shard_map/pallas_call | solution.py:512
  90.9 58.6 %shard_map.113 = (bf16[128,7168]{1,0:T(8,128)(2,1)}, f32[8,128]{1,0:T(8,128)}, bf16[128,7168]{1,0:T(8,128)(2,1)}) custom-call(f32[8,128]{1,0:T(8,128)} %bitcast.5, s32[8,128]{1,0:T(8,128)} %bitcast.7, s32[8,128]{1,0:T(8,128)} %bitcast.9, f32[4,2,8,1024]{3,2,1,0:T(8,128)} %get-tuple-element.8.yr_ref, bf16[12,2,64,640]{3,2,1,0:T(8,128)(2,1)} %get-tuple-element.9.dg), custom_call_target="tpu_custom_call" | custom-call | tf_op jit(solution)/shard_map/pallas_call | solution.py:525

commit v2 on v1

--- a/solution.py
+++ b/solution.py
@@ -19,7 +19,7 @@
 NX = EXPERTS
 NY = 8
 NZ = 12
-SPAN = 640
+SPANS = (384, 256)
 
 
 def iota(shape, dim):
@@ -73,10 +73,10 @@
 
 def main_kernel(
     logits_ref, group_ref, member_ref, sg_ref, su_ref, cot_hbm, gate_hbm, up_hbm, down_hbm,
-    yr, dg,
-    cotv, downv, guv, xs, xr, av, w2, hv, gp, upv, own, qs, qr, p0, p1, sm0, sm1, rm0, rm1, ys,
+    yr, dg0, dg1,
+    cotv, downv, guv, xs, xr, av, w20, w21, hv, gp, upv, own0, own1, qs, qr, p0, p1, sm0, sm1, rm0, rm1, ys,
     load_sem,
-    xs_s, xs_r, za_s, za_r, a_s, a_r, as_s, as_r, b_s, b_r, bs_s, bs_r, h_s, h_r, o_s, o_r,
+    xs_s, xs_r, za_s, za_r, a_s, a_r, as_s, as_r, b_s, b_r, bs_s, bs_r, c_s, c_r, cs_s, cs_r, h_s, h_r, o_s, o_r,
     q_s, q_r, m_s, m_r, y_s, y_r, loc,
 ):
     e = lax.axis_index("expert")
@@ -115,12 +115,6 @@
 
     for j in range(8):
         load(cot_hbm.at[:, pl.ds(j * seg, seg)], cotv.at[j], j)
-    for j in range(4):
-        load(down_hbm.at[:, pl.ds(j * subw, subw)], downv.at[j], 8 + j)
-    for j in range(8):
-        load(gate_hbm.at[pl.ds(j * seg, seg), :], guv.at[j, :, pl.ds(0, 128)], 12 + j)
-        load(up_hbm.at[pl.ds(j * seg, seg), :], guv.at[j, :, pl.ds(128, 128)], 20 + j)
-
     barrier = pltpu.get_barrier_semaphore()
     greeted = 0
 
@@ -149,9 +143,7 @@
         gate_pre = gp[...]
         hidden = (gate_pre * jax.nn.sigmoid(gate_pre) * upv[...]).astype(bf16)
         zz = z // 2
-        hv[z % 2, zz // 3, :, zz % 3] = hidden.reshape(NY, 16, 128)
-
-    own_hidden()
+        hv[z % 2, :, zz] = hidden.reshape(NY, 16, 128)
 
     affinity, affinity_sum, hits, slot8, gate8 = routing(logits_ref[...], group_ref[...], member_ref[...])
     rows64 = mm(expand_rows(64), (slot8 * gate8).astype(bf16))
@@ -166,33 +158,20 @@
 
     pl.semaphore_wait(barrier, greeted)
 
-    h_steps = [(0, t) for t in range(NZ // 2)] + [(1, t) for t in range(NZ // 2 - 1)]
-
-    def hchunk(zz):
-        return hv.at[zz % 2, (zz // 2) // 3, :, (zz // 2) % 3]
-
-    def h_send(d, t):
-        s = 1 if d == 0 else -1
-        ref = hchunk((z - s * t + NZ) % NZ)
-        k = d * (NZ // 2) + t
-        send(ref, ref, h_s.at[k], h_r.at[k], at((z + s + NZ) % NZ, x, y, c))
-
-    def h_recv(d, t):
-        s = 1 if d == 0 else -1
-        arrived(hchunk((z - s * (t + 1) + NZ) % NZ), h_r.at[d * (NZ // 2) + t])
-        if (d, t + 1) in h_steps:
-            h_send(d, t + 1)
-
     keep = pltpu.make_async_copy(xs.at[x, c], xr.at[x, c], xs_r.at[x * 2 + c])
-    for dx in range(NX):
+    for dx in (2, 1, 3, 0):
         for dc in range(2):
             if dx == 0 and dc == 0:
                 keep.start()
                 continue
             xx, cc = (x + dx) % NX, (c + dc) % 2
             send(xs.at[xx, cc], xr.at[x, c], xs_s.at[dx * 2 + dc], xs_r.at[x * 2 + c], at(z, xx, y, cc))
-    h_send(0, 0)
-    h_send(1, 0)
+    for j in range(4):
+        load(down_hbm.at[:, pl.ds(j * subw, subw)], downv.at[j], 8 + j)
+    for j in range(8):
+        load(gate_hbm.at[pl.ds(j * seg, seg), :], guv.at[j, :, pl.ds(0, 128)], 12 + j)
+        load(up_hbm.at[pl.ds(j * seg, seg), :], guv.at[j, :, pl.ds(128, 128)], 20 + j)
+    own_hidden()
     for xx in range(NX):
         for cc in range(2):
             arrived(xr.at[xx, cc], xs_r.at[xx * 2 + cc])
@@ -203,122 +182,129 @@
         pick = one_hot(((k16 // 8) * CAP + k16 % CAP == i16) & ((k16 // CAP) % 4 == s))
         av[c, s // 2, y, :, pl.ds((s % 2) * seg, seg)] = mm(pick, got).astype(bf16)
 
-    def ring(buf, ssem, rsem, sib_s, sib_r):
-        steps = {(d, s): (NY // 2 if d == s else NY // 2 - 1) for d in range(2) for s in range(2)}
-
-        def number(d, s, t):
-            return (d * 2 + s) * (NY // 2) + t
-
-        def put(d, s, t):
+    def ring(chunk, longer, ssem, rsem, sib_s, sib_r):
+        steps = [NY // 2 if d == longer else NY // 2 - 1 for d in range(2)]
+
+        def put(d, t):
             g = 1 if d == 0 else -1
-            ref = buf.at[c, s, (y - g * t + NY) % NY]
-            k = number(d, s, t)
+            ref = chunk(c, (y - g * t + NY) % NY)
+            k = d * (NY // 2) + t
             send(ref, ref, ssem.at[k], rsem.at[k], at(z, x, (y + g + NY) % NY, c))
 
-        def across(yy, s, k):
-            ref = buf.at[c, s, yy]
+        def across(yy, k):
+            ref = chunk(c, yy)
             send(ref, ref, sib_s.at[k], sib_r.at[k], at(z, x, y, other))
 
         def first():
-            for s in range(2):
-                put(0, s, 0)
-                put(1, s, 0)
-            for s in range(2):
-                across(y, s, 16 + s)
+            put(0, 0)
+            put(1, 0)
+            across(y, NY)
 
         def turn(t):
-            for s in range(2):
-                for d in range(2):
-                    if t < steps[d, s]:
-                        g = 1 if d == 0 else -1
-                        yy = (y - g * (t + 1) + NY) % NY
-                        k = number(d, s, t)
-                        arrived(buf.at[c, s, yy], rsem.at[k])
-                        if t + 1 < steps[d, s]:
-                            put(d, s, t + 1)
-                        across(yy, s, k)
+            for d in range(2):
+                if t < steps[d]:
+                    g = 1 if d == 0 else -1
+                    yy = (y - g * (t + 1) + NY) % NY
+                    k = d * (NY // 2) + t
+                    arrived(chunk(c, yy), rsem.at[k])
+                    if t + 1 < steps[d]:
+                        put(d, t + 1)
+                    across(yy, k)
 
         def last():
-            for s in range(2):
-                arrived(buf.at[other, s, y], sib_r.at[16 + s])
-                for d in range(2):
-                    g = 1 if d == 0 else -1
-                    for t in range(steps[d, s]):
-                        yy = (y - g * (t + 1) + NY) % NY
-                        arrived(buf.at[other, s, yy], sib_r.at[number(d, s, t)])
+            arrived(chunk(other, y), sib_r.at[NY])
+            for d in range(2):
+                g = 1 if d == 0 else -1
+                for t in range(steps[d]):
+                    arrived(chunk(other, (y - g * (t + 1) + NY) % NY), sib_r.at[d * (NY // 2) + t])
 
         return first, turn, last
 
-    a_first, a_turn, a_last = ring(av, a_s, a_r, as_s, as_r)
-    b_first, b_turn, b_last = ring(w2, b_s, b_r, bs_s, bs_r)
-    a_first()
-
-    def first_tile(k):
-        return (14 * k) // 3
+    a_rings = [
+        ring(lambda cc, yy, s=s: av.at[cc, s, yy], s, a_s.at[s], a_r.at[s], as_s.at[s], as_r.at[s]) for s in range(2)
+    ]
+    b_first, b_turn, b_last = ring(lambda cc, yy: w20.at[cc, yy], 0, b_s, b_r, bs_s, bs_r)
+    c_first, c_turn, c_last = ring(lambda cc, yy: w21.at[cc, yy], 1, c_s, c_r, cs_s, cs_r)
+    for first, _, _ in a_rings:
+        first()
 
     zq = z // 2
     per_half = NZ // 2
-    for k in range(per_half):
-        zz = c * per_half + k
-        start = first_tile(k) * 128
-        src = av.at[c, start // subw, y, :, pl.ds(start % subw, SPAN)]
-        dst = w2.at[z % 2, zq // 3, y, zq % 3]
-        copy = pltpu.make_async_remote_copy(
-            src_ref=src, dst_ref=dst, send_sem=za_s.at[k], recv_sem=za_r.at[zq],
-            device_id=at(zz, x, y, z % 2), device_id_type=MESH,
-        )
-        here = pltpu.make_async_copy(src, dst, za_r.at[zq])
-        remote = jnp.logical_or(zz != z, z % 2 != c)
-
-        @pl.when(remote)
-        def _(copy=copy):
-            copy.start()
-
-        @pl.when(jnp.logical_not(remote))
-        def _(here=here):
-            here.start()
-        pending.append((copy, remote))
+    for part, w2 in enumerate((w20, w21)):
+        span = SPANS[part]
+        for k in range(per_half):
+            zz = c * per_half + k
+            start = (14 * k) // 3 * 128
+            src = av.at[c, start // subw, y, :, pl.ds(start % subw + part * SPANS[0], span)]
+            dst = w2.at[z % 2, y, zq]
+            copy = pltpu.make_async_remote_copy(
+                src_ref=src, dst_ref=dst, send_sem=za_s.at[part, k], recv_sem=za_r.at[part, zq],
+                device_id=at(zz, x, y, z % 2), device_id_type=MESH,
+            )
+            here = pltpu.make_async_copy(src, dst, za_r.at[part, zq])
+            remote = jnp.logical_or(zz != z, z % 2 != c)
+
+            @pl.when(remote)
+            def _(copy=copy):
+                copy.start()
+
+            @pl.when(jnp.logical_not(remote))
+            def _(here=here):
+                here.start()
+            pending.append((copy, remote))
+    for dz in range(1, NZ):
+        ref = hv.at[z % 2, :, zq]
+        send(ref, ref, h_s.at[dz], h_r.at[dz], at((z + dz) % NZ, x, y, c))
     for q in range(NZ // 2):
-        arrived(w2.at[c, q // 3, y, q % 3], za_r.at[q])
+        arrived(w20.at[c, y, q], za_r.at[0, q])
     b_first()
+    for q in range(NZ // 2):
+        arrived(w21.at[c, y, q], za_r.at[1, q])
+    c_first()
 
     for t in range(NY // 2):
-        a_turn(t)
+        for _, turn, _ in a_rings:
+            turn(t)
         b_turn(t)
-        for k in (t * 2, t * 2 + 1):
-            for d in range(2):
-                if (d, k) in h_steps:
-                    h_recv(d, k)
+        if t:
+            c_turn(t - 1)
     b_last()
-
-    mine = mm(hv[...].reshape(-1, 128), w2[...].reshape(-1, SPAN), 0, 0).astype(bf16)
-    own[...] = mine.reshape(2, 64, SPAN)
-    keep_out = pltpu.make_async_copy(own, dg.at[z], loc.at[0])
-    keep_out.start()
+    for dz in range(1, NZ):
+        zz = (z - dz + NZ) % NZ
+        arrived(hv.at[zz % 2, :, zz // 2], h_r.at[dz])
+
     o_steps = {(d, s): (NZ // 2 if d == s else NZ // 2 - 1) for d in range(2) for s in range(2)}
+    owns, dgs, keeps = (own0, own1), (dg0, dg1), []
 
     def o_send(d, s, t):
         g = 1 if d == 0 else -1
         zz = (z - g * t + NZ) % NZ
         k = (d * 2 + s) * (NZ // 2) + t
-        src = own.at[s] if t == 0 else dg.at[zz, s]
-        send(src, dg.at[zz, s], o_s.at[k], o_r.at[k], at((z + g + NZ) % NZ, x, y, c))
-
-    def o_turn(t):
-        for s in range(2):
-            for d in range(2):
-                if t < o_steps[d, s]:
-                    g = 1 if d == 0 else -1
-                    k = (d * 2 + s) * (NZ // 2) + t
-                    arrived(dg.at[(z - g * (t + 1) + NZ) % NZ, s], o_r.at[k])
-                    if t + 1 < o_steps[d, s]:
-                        o_send(d, s, t + 1)
-
-    for s in range(2):
+        src = owns[s] if t == 0 else dgs[s].at[zz]
+        send(src, dgs[s].at[zz], o_s.at[k], o_r.at[k], at((z + g + NZ) % NZ, x, y, c))
+
+    def o_turn(s, t):
+        for d in range(2):
+            if t < o_steps[d, s]:
+                g = 1 if d == 0 else -1
+                k = (d * 2 + s) * (NZ // 2) + t
+                arrived(dgs[s].at[(z - g * (t + 1) + NZ) % NZ], o_r.at[k])
+                if t + 1 < o_steps[d, s]:
+                    o_send(d, s, t + 1)
+
+    def down(s):
+        w2 = (w20, w21)[s]
+        owns[s][...] = mm(hv[...].reshape(-1, 128), w2[...].reshape(-1, SPANS[s]), 0, 0).astype(bf16)
+        copy = pltpu.make_async_copy(owns[s], dgs[s].at[z], loc.at[s])
+        copy.start()
+        keeps.append(copy)
         o_send(0, s, 0)
         o_send(1, s, 0)
 
-    a_last()
+    down(0)
+
+    for _, _, last in a_rings:
+        last()
     for j in range(8, 28):
         loads[j].wait()
     grad_hidden = mm(av[0, 0].reshape(128, subw), downv[0], 1, 1)
@@ -333,6 +319,9 @@
     grad_gate = (grad_hidden * up_pre * sig * (1.0 + gate_pre * (1.0 - sig))).astype(bf16)
     grad_up = (grad_hidden * act).astype(bf16)
     both = jnp.concatenate([grad_gate, grad_up], axis=1)
+    c_turn(NY // 2 - 1)
+    c_last()
+    down(1)
     for s in range(4):
         qs[s] = mm(both, guv[other * 4 + s], 1, 1).astype(bf16)
         send(qs.at[s], qr.at[s], q_s.at[s], q_r.at[s], at(z, x, y, other))
@@ -372,7 +361,8 @@
                     arrived(rm[s].at[n], m_r.at[s * 8 + n])
                     if t + 1 < m_steps[d, s]:
                         m_send(d, s, t + 1)
-        o_turn(t)
+        o_turn(0, t)
+        o_turn(1, t)
 
     i64 = iota((64, 16), 0)
     k64 = iota((64, 16), 1)
@@ -403,11 +393,13 @@
             xx, cc = (x + dx) % NX, (c + dc) % 2
             send(ys.at[xx, cc], yr.at[x, c], y_s.at[dx * 2 + dc], y_r.at[x * 2 + c], at(z, xx, y, cc))
     for t in range(NY // 2, NZ // 2):
-        o_turn(t)
+        o_turn(0, t)
+        o_turn(1, t)
     for xx in range(NX):
         for cc in range(2):
             arrived(yr.at[xx, cc], y_r.at[xx * 2 + cc])
-    keep_out.wait()
+    for copy in keeps:
+        copy.wait()
     for item in pending:
         if isinstance(item, tuple):
             copy, cond = item
@@ -420,24 +412,14 @@
 
 
 def final_kernel(
-    logits_ref, group_ref, member_ref, yr_ref, dg, token_out, logit_ref, down_out, stage, sems
+    logits_ref, group_ref, member_ref, yr_ref, dg0, dg1, token_out, logit_ref, down_out, stage, in0, in1, sems, down_sems
 ):
     seg = stage.shape[2]
     per_half = NZ // 2
     copies = []
-    for zz in range(NZ):
-        k = zz % per_half
-        start = (14 * k) // 3
-        width = ((14 * (k + 1)) // 3 - start) * 128
-        start = (zz // per_half) * 4 * seg + start * 128
-        for s in range(2):
-            copy = pltpu.make_async_copy(
-                dg.at[zz, s, :, pl.ds(0, width)],
-                down_out.at[pl.ds(s * 64, 64), pl.ds(start, width)],
-                sems.at[8 + zz * 2 + s],
-            )
-            copy.start()
-            copies.append(copy)
+    fetch = [pltpu.make_async_copy(dg0, in0, sems.at[8]), pltpu.make_async_copy(dg1, in1, sems.at[9])]
+    for copy in fetch:
+        copy.start()
     affinity, affinity_sum, hits, slot8, gate8 = routing(logits_ref[...], group_ref[...], member_ref[...])
     grads = yr_ref[:, :, :, 0:seg].reshape(64, seg)
     pieces = jnp.concatenate(split(grads), axis=0)
@@ -450,6 +432,21 @@
         copy = pltpu.make_async_copy(stage.at[j], token_out.at[:, pl.ds(j * seg, seg)], sems.at[j])
         copy.start()
         copies.append(copy)
+    for s, part in enumerate((in0, in1)):
+        fetch[s].wait()
+        for zz in range(NZ):
+            k = zz % per_half
+            start = (14 * k) // 3
+            end = (14 * (k + 1)) // 3
+            low = start * 128 + s * SPANS[0]
+            width = min(SPANS[s], end * 128 - low)
+            copy = pltpu.make_async_copy(
+                part.at[zz, :, pl.ds(0, width)],
+                down_out.at[:, pl.ds((zz // per_half) * 4 * seg + low, width)],
+                down_sems.at[zz * 2 + s],
+            )
+            copy.start()
+            copies.append(copy)
     products = yr_ref[:, :, :, seg:seg + 128].reshape(64, 128)
     folded = jnp.zeros((8, 128), f32)
     for piece in split(products):
@@ -483,11 +480,13 @@
         pltpu.VMEM((NX, 2, 8, seg), f32),
         pltpu.VMEM((NX, 2, 8, seg), f32),
         pltpu.VMEM((2, 2, NY, 16, subw), bf16),
-        pltpu.VMEM((2, 2, NY, 3, 16, SPAN), bf16),
-        pltpu.VMEM((2, 2, NY, 3, 16, 128), bf16),
+        pltpu.VMEM((2, NY, NZ // 2, 16, SPANS[0]), bf16),
+        pltpu.VMEM((2, NY, NZ // 2, 16, SPANS[1]), bf16),
+        pltpu.VMEM((2, NY, NZ // 2, 16, 128), bf16),
         pltpu.VMEM((128, 128), f32),
         pltpu.VMEM((128, 128), f32),
-        pltpu.VMEM((2, 64, SPAN), bf16),
+        pltpu.VMEM((128, SPANS[0]), bf16),
+        pltpu.VMEM((128, SPANS[1]), bf16),
         pltpu.VMEM((4, 128, seg), bf16),
         pltpu.VMEM((4, 128, seg), bf16),
         pltpu.VMEM((NY, 16, subw), f32),
@@ -499,24 +498,26 @@
         pltpu.VMEM((NX, 2, 8, seg + 128), f32),
         dma((28,)),
         dma((8,)), dma((8,)),
-        dma((6,)), dma((6,)),
-        dma((16,)), dma((16,)), dma((18,)), dma((18,)),
-        dma((16,)), dma((16,)), dma((18,)), dma((18,)),
+        dma((2, 6)), dma((2, 6)),
+        dma((2, 8)), dma((2, 8)), dma((2, 9)), dma((2, 9)),
+        dma((8,)), dma((8,)), dma((9,)), dma((9,)),
+        dma((8,)), dma((8,)), dma((9,)), dma((9,)),
         dma((12,)), dma((12,)),
         dma((24,)), dma((24,)),
         dma((4,)), dma((4,)),
         dma((16,)), dma((16,)),
         dma((8,)), dma((8,)),
-        dma((1,)),
+        dma((2,)),
     ]
-    yr, dg = pl.pallas_call(
+    yr, dg0, dg1 = pl.pallas_call(
         main_kernel,
         out_shape=(
             jax.ShapeDtypeStruct((NX, 2, 8, seg + 128), f32),
-            jax.ShapeDtypeStruct((NZ, 2, 64, SPAN), bf16),
+            jax.ShapeDtypeStruct((NZ, 128, SPANS[0]), bf16),
+            jax.ShapeDtypeStruct((NZ, 128, SPANS[1]), bf16),
         ),
         in_specs=[vmem] * 5 + [hbm] * 4,
-        out_specs=(hbm, hbm),
+        out_specs=(hbm, hbm, hbm),
         scratch_shapes=scratch,
         compiler_params=pltpu.CompilerParams(
             collective_id=0, has_side_effects=True, vmem_limit_bytes=62 * 1024 * 1024
@@ -529,11 +530,17 @@
             jax.ShapeDtypeStruct((8, tokens), f32),
             jax.ShapeDtypeStruct((128, width), bf16),
         ),
-        in_specs=[vmem] * 4 + [hbm],
+        in_specs=[vmem] * 4 + [hbm] * 2,
         out_specs=(hbm, vmem, hbm),
-        scratch_shapes=[pltpu.VMEM((8, tokens, seg), bf16), dma((32,))],
+        scratch_shapes=[
+            pltpu.VMEM((8, tokens, seg), bf16),
+            pltpu.VMEM((NZ, 128, SPANS[0]), bf16),
+            pltpu.VMEM((NZ, 128, SPANS[1]), bf16),
+            dma((10,)),
+            dma((24,)),
+        ],
         compiler_params=pltpu.CompilerParams(vmem_limit_bytes=62 * 1024 * 1024),
-    )(logits_t, group_t, member_t, yr, dg)
+    )(logits_t, group_t, member_t, yr, dg0, dg1)
     return token_grad, logit_grad.T, down_grad
 
 

time: 152 us -> 97.8 us (0.64)
  Pallas kernels: 149 us -> 95.5 us
    pallas_call x1, Pallas kernels: 58.6 us -> 4.37 us  [body(): pl.pallas_call(final_kernel, out_shape=(jax.ShapeDtypeStruct((tokens, wid...]
where the time goes in v2:
time: 97.8 us; the launch traced here: 96.2 us
  Pallas kernels  95.5 us (98%)
    pallas_call x1, Pallas kernels, body(): pl.pallas_call(main_kernel, out_shape=(jax.ShapeDtypeStruct((NX, 2, 8, se...  91.2 us
    pallas_call x1, Pallas kernels, body(): pl.pallas_call(final_kernel, out_shape=(jax.ShapeDtypeStruct((tokens, wid...  4.37 us

profile of v2, /device:TPU:6, one launch (start us, length us, event | category | flops | bytes accessed | tf_op | source)
XLA Modules:
  0.0 96.2 jit_solution(9649632578975035553)
XLA Ops:
  0.6 91.2 %shard_map.112 = (f32[4,2,8,1024]{3,2,1,0:T(8,128)}, bf16[12,128,384]{2,1,0:T(8,128)(2,1)}, bf16[12,128,256]{2,1,0:T(8,128)(2,1)}) custom-call(f32[8,128]{1,0:T(8,128)} %bitcast.4, s32[8,128]{1,0:T(8,128)} %bitcast.6, s32[8,128]{1,0:T(8,128)} %bitcast.8, bf16[128,128]{1,0:T(8,128)(2,1)} %sg_ref.1, bf16[128,128]{1,0:T(8,128)(2,1)} %su_ref.1, ...), custom_call_target="tpu_custom_call" | custom-call | tf_op jit(solution)/shard_map/pallas_call | solution.py:512
  91.8 4.4 %shard_map.113 = (bf16[128,7168]{1,0:T(8,128)(2,1)}, f32[8,128]{1,0:T(8,128)}, bf16[128,7168]{1,0:T(8,128)(2,1)}) custom-call(f32[8,128]{1,0:T(8,128)} %bitcast.5, s32[8,128]{1,0:T(8,128)} %bitcast.7, s32[8,128]{1,0:T(8,128)} %bitcast.9, f32[4,2,8,1024]{3,2,1,0:T(8,128)} %get-tuple-element.9.yr_ref, bf16[12,128,384]{2,1,0:T(8,128)(2,1)} %get-tuple-element.10.dg0, ...), custom_call_target="tpu_custom_call" | custom-call | tf_op jit(solution)/shard_map/pallas_call | solution.py:526

commit v3 on v1

--- a/solution.py
+++ b/solution.py
@@ -20,6 +20,7 @@
 NY = 8
 NZ = 12
 SPAN = 640
+TILES = SPAN // 128
 
 
 def iota(shape, dim):
@@ -74,7 +75,8 @@
 def main_kernel(
     logits_ref, group_ref, member_ref, sg_ref, su_ref, cot_hbm, gate_hbm, up_hbm, down_hbm,
     yr, dg,
-    cotv, downv, guv, xs, xr, av, w2, hv, gp, upv, own, qs, qr, p0, p1, sm0, sm1, rm0, rm1, ys,
+    cotv, downv, guv, xs, xr, av, w2, hv, gp, upv, ov, qs, qr, p0, p1, p2, p3,
+    sm0, sm1, sm2, sm3, rm0, rm1, rm2, rm3, ys,
     load_sem,
     xs_s, xs_r, za_s, za_r, a_s, a_r, as_s, as_r, b_s, b_r, bs_s, bs_r, h_s, h_r, o_s, o_r,
     q_s, q_r, m_s, m_r, y_s, y_r, loc,
@@ -115,12 +117,6 @@
 
     for j in range(8):
         load(cot_hbm.at[:, pl.ds(j * seg, seg)], cotv.at[j], j)
-    for j in range(4):
-        load(down_hbm.at[:, pl.ds(j * subw, subw)], downv.at[j], 8 + j)
-    for j in range(8):
-        load(gate_hbm.at[pl.ds(j * seg, seg), :], guv.at[j, :, pl.ds(0, 128)], 12 + j)
-        load(up_hbm.at[pl.ds(j * seg, seg), :], guv.at[j, :, pl.ds(128, 128)], 20 + j)
-
     barrier = pltpu.get_barrier_semaphore()
     greeted = 0
 
@@ -149,9 +145,7 @@
         gate_pre = gp[...]
         hidden = (gate_pre * jax.nn.sigmoid(gate_pre) * upv[...]).astype(bf16)
         zz = z // 2
-        hv[z % 2, zz // 3, :, zz % 3] = hidden.reshape(NY, 16, 128)
-
-    own_hidden()
+        hv[z % 2, :, zz] = hidden.reshape(NY, 16, 128)
 
     affinity, affinity_sum, hits, slot8, gate8 = routing(logits_ref[...], group_ref[...], member_ref[...])
     rows64 = mm(expand_rows(64), (slot8 * gate8).astype(bf16))
@@ -166,33 +160,40 @@
 
     pl.semaphore_wait(barrier, greeted)
 
-    h_steps = [(0, t) for t in range(NZ // 2)] + [(1, t) for t in range(NZ // 2 - 1)]
-
-    def hchunk(zz):
-        return hv.at[zz % 2, (zz // 2) // 3, :, (zz // 2) % 3]
-
-    def h_send(d, t):
-        s = 1 if d == 0 else -1
-        ref = hchunk((z - s * t + NZ) % NZ)
-        k = d * (NZ // 2) + t
-        send(ref, ref, h_s.at[k], h_r.at[k], at((z + s + NZ) % NZ, x, y, c))
-
-    def h_recv(d, t):
-        s = 1 if d == 0 else -1
-        arrived(hchunk((z - s * (t + 1) + NZ) % NZ), h_r.at[d * (NZ // 2) + t])
-        if (d, t + 1) in h_steps:
-            h_send(d, t + 1)
-
     keep = pltpu.make_async_copy(xs.at[x, c], xr.at[x, c], xs_r.at[x * 2 + c])
-    for dx in range(NX):
+    for dx in (2, 1, 3, 0):
         for dc in range(2):
             if dx == 0 and dc == 0:
                 keep.start()
                 continue
             xx, cc = (x + dx) % NX, (c + dc) % 2
             send(xs.at[xx, cc], xr.at[x, c], xs_s.at[dx * 2 + dc], xs_r.at[x * 2 + c], at(z, xx, y, cc))
+    for j in range(4):
+        load(down_hbm.at[:, pl.ds(j * subw, subw)], downv.at[j], 8 + j)
+    for j in range(8):
+        load(gate_hbm.at[pl.ds(j * seg, seg), :], guv.at[j, :, pl.ds(0, 128)], 12 + j)
+        load(up_hbm.at[pl.ds(j * seg, seg), :], guv.at[j, :, pl.ds(128, 128)], 20 + j)
+    own_hidden()
+
+    def h_send(d, t):
+        g = 1 if d == 0 else -1
+        zz = (z - g * t + NZ) % NZ
+        ref = hv.at[zz % 2, :, zz // 2]
+        k = d * (NZ // 2) + t
+        send(ref, ref, h_s.at[k], h_r.at[k], at((z + g + NZ) % NZ, x, y, c))
+
+    def h_turn(t):
+        for d in range(2):
+            if t < NZ // 2 - d:
+                g = 1 if d == 0 else -1
+                zz = (z - g * (t + 1) + NZ) % NZ
+                arrived(hv.at[zz % 2, :, zz // 2], h_r.at[d * (NZ // 2) + t])
+                if t + 1 < NZ // 2 - d:
+                    h_send(d, t + 1)
+
     h_send(0, 0)
     h_send(1, 0)
+    h_turn(0)
     for xx in range(NX):
         for cc in range(2):
             arrived(xr.at[xx, cc], xs_r.at[xx * 2 + cc])
@@ -203,66 +204,53 @@
         pick = one_hot(((k16 // 8) * CAP + k16 % CAP == i16) & ((k16 // CAP) % 4 == s))
         av[c, s // 2, y, :, pl.ds((s % 2) * seg, seg)] = mm(pick, got).astype(bf16)
 
-    def ring(buf, ssem, rsem, sib_s, sib_r):
-        steps = {(d, s): (NY // 2 if d == s else NY // 2 - 1) for d in range(2) for s in range(2)}
-
-        def number(d, s, t):
-            return (d * 2 + s) * (NY // 2) + t
-
-        def put(d, s, t):
+    def ring(chunk, longer, ssem, rsem):
+        steps = [NY // 2 if d == longer else NY // 2 - 1 for d in range(2)]
+
+        def put(d, t):
             g = 1 if d == 0 else -1
-            ref = buf.at[c, s, (y - g * t + NY) % NY]
-            k = number(d, s, t)
+            ref = chunk((y - g * t + NY) % NY)
+            k = d * (NY // 2) + t
             send(ref, ref, ssem.at[k], rsem.at[k], at(z, x, (y + g + NY) % NY, c))
 
-        def across(yy, s, k):
-            ref = buf.at[c, s, yy]
-            send(ref, ref, sib_s.at[k], sib_r.at[k], at(z, x, y, other))
-
-        def first():
-            for s in range(2):
-                put(0, s, 0)
-                put(1, s, 0)
-            for s in range(2):
-                across(y, s, 16 + s)
-
-        def turn(t):
-            for s in range(2):
-                for d in range(2):
-                    if t < steps[d, s]:
-                        g = 1 if d == 0 else -1
-                        yy = (y - g * (t + 1) + NY) % NY
-                        k = number(d, s, t)
-                        arrived(buf.at[c, s, yy], rsem.at[k])
-                        if t + 1 < steps[d, s]:
-                            put(d, s, t + 1)
-                        across(yy, s, k)
-
-        def last():
-            for s in range(2):
-                arrived(buf.at[other, s, y], sib_r.at[16 + s])
-                for d in range(2):
-                    g = 1 if d == 0 else -1
-                    for t in range(steps[d, s]):
-                        yy = (y - g * (t + 1) + NY) % NY
-                        arrived(buf.at[other, s, yy], sib_r.at[number(d, s, t)])
-
-        return first, turn, last
-
-    a_first, a_turn, a_last = ring(av, a_s, a_r, as_s, as_r)
-    b_first, b_turn, b_last = ring(w2, b_s, b_r, bs_s, bs_r)
-    a_first()
-
-    def first_tile(k):
-        return (14 * k) // 3
+        def turn(d, t):
+            if t < steps[d]:
+                g = 1 if d == 0 else -1
+                arrived(chunk((y - g * (t + 1) + NY) % NY), rsem.at[d * (NY // 2) + t])
+                if t + 1 < steps[d]:
+                    put(d, t + 1)
+
+        return put, turn
+
+    def whose(d, t):
+        return (y - (1 if d == 0 else -1) * (t + 1) + NY) % NY
+
+    a_rings = [ring(lambda yy, s=s: av.at[c, s, yy], s, a_s.at[s], a_r.at[s]) for s in range(2)]
+
+    def a_across(s, yy, k):
+        ref = av.at[c, s, yy]
+        send(ref, ref, as_s.at[s, k], as_r.at[s, k], at(z, x, y, other))
+
+    def a_turn(t):
+        for s in range(2):
+            for d in range(2):
+                a_rings[s][1](d, t)
+                if t < NY // 2 - (d != s):
+                    a_across(s, whose(d, t), d * (NY // 2) + t)
+
+    for put, _ in a_rings:
+        put(0, 0)
+        put(1, 0)
+    for s in range(2):
+        a_across(s, y, NY)
 
     zq = z // 2
     per_half = NZ // 2
     for k in range(per_half):
         zz = c * per_half + k
-        start = first_tile(k) * 128
+        start = (14 * k) // 3 * 128
         src = av.at[c, start // subw, y, :, pl.ds(start % subw, SPAN)]
-        dst = w2.at[z % 2, zq // 3, y, zq % 3]
+        dst = w2.at[z % 2, y, zq]
         copy = pltpu.make_async_remote_copy(
             src_ref=src, dst_ref=dst, send_sem=za_s.at[k], recv_sem=za_r.at[zq],
             device_id=at(zz, x, y, z % 2), device_id_type=MESH,
@@ -278,47 +266,51 @@
         def _(here=here):
             here.start()
         pending.append((copy, remote))
-    for q in range(NZ // 2):
-        arrived(w2.at[c, q // 3, y, q % 3], za_r.at[q])
-    b_first()
-
-    for t in range(NY // 2):
-        a_turn(t)
-        b_turn(t)
-        for k in (t * 2, t * 2 + 1):
+    h_turn(1)
+    a_turn(0)
+    h_turn(2)
+
+    b_rings = []
+    order = (0, 1, -1, 2, -2, 3)
+    for n, r in enumerate(order):
+        q = (zq + r + NZ // 2) % (NZ // 2)
+        put, turn = ring(lambda yy, q=q: w2.at[c, yy, q], n % 2, b_s.at[n], b_r.at[n])
+        b_rings.append((put, turn))
+        arrived(w2.at[c, y, q], za_r.at[q])
+        put(0, 0)
+        put(1, 0)
+
+    def b_across(yy, k):
+        ref = w2.at[c, yy]
+        send(ref, ref, bs_s.at[k], bs_r.at[k], at(z, x, y, other))
+
+    b_across(y, NY)
+
+    def b_turn(t):
+        for _, turn in b_rings:
             for d in range(2):
-                if (d, k) in h_steps:
-                    h_recv(d, k)
-    b_last()
-
-    mine = mm(hv[...].reshape(-1, 128), w2[...].reshape(-1, SPAN), 0, 0).astype(bf16)
-    own[...] = mine.reshape(2, 64, SPAN)
-    keep_out = pltpu.make_async_copy(own, dg.at[z], loc.at[0])
-    keep_out.start()
-    o_steps = {(d, s): (NZ // 2 if d == s else NZ // 2 - 1) for d in range(2) for s in range(2)}
-
-    def o_send(d, s, t):
-        g = 1 if d == 0 else -1
-        zz = (z - g * t + NZ) % NZ
-        k = (d * 2 + s) * (NZ // 2) + t
-        src = own.at[s] if t == 0 else dg.at[zz, s]
-        send(src, dg.at[zz, s], o_s.at[k], o_r.at[k], at((z + g + NZ) % NZ, x, y, c))
-
-    def o_turn(t):
-        for s in range(2):
+                turn(d, t)
+        if t < NY // 2 - 1:
             for d in range(2):
-                if t < o_steps[d, s]:
-                    g = 1 if d == 0 else -1
-                    k = (d * 2 + s) * (NZ // 2) + t
-                    arrived(dg.at[(z - g * (t + 1) + NZ) % NZ, s], o_r.at[k])
-                    if t + 1 < o_steps[d, s]:
-                        o_send(d, s, t + 1)
+                b_across(whose(d, t), d * (NY // 2) + t)
+        else:
+            b_across(whose(0, t), t)
+
+    h_turn(3)
+    a_turn(1)
+    b_turn(0)
+    h_turn(4)
+    a_turn(2)
+    b_turn(1)
+    h_turn(5)
+    a_turn(3)
+    b_turn(2)
 
     for s in range(2):
-        o_send(0, s, 0)
-        o_send(1, s, 0)
-
-    a_last()
+        arrived(av.at[other, s, y], as_r.at[s, NY])
+        for d in range(2):
+            for t in range(NY // 2 - (d != s)):
+                arrived(av.at[other, s, whose(d, t)], as_r.at[s, d * (NY // 2) + t])
     for j in range(8, 28):
         loads[j].wait()
     grad_hidden = mm(av[0, 0].reshape(128, subw), downv[0], 1, 1)
@@ -329,19 +321,75 @@
     sig = jax.nn.sigmoid(gate_pre)
     act = gate_pre * sig
     hidden = (act * up_pre).astype(bf16).astype(f32)
-    p1[:, :, pl.ds(subw, 128)] = (hidden * grad_hidden).reshape(NY, 16, 128)
+    p3[:, :, pl.ds(seg, 128)] = (hidden * grad_hidden).reshape(NY, 16, 128)
     grad_gate = (grad_hidden * up_pre * sig * (1.0 + gate_pre * (1.0 - sig))).astype(bf16)
     grad_up = (grad_hidden * act).astype(bf16)
     both = jnp.concatenate([grad_gate, grad_up], axis=1)
     for s in range(4):
         qs[s] = mm(both, guv[other * 4 + s], 1, 1).astype(bf16)
         send(qs.at[s], qr.at[s], q_s.at[s], q_r.at[s], at(z, x, y, other))
+    b_turn(3)
+    pp, sm, rm = (p0, p1, p2, p3), (sm0, sm1, sm2, sm3), (rm0, rm1, rm2, rm3)
     for s in range(4):
-        part = mm(both, guv[c * 4 + s], 1, 1)
-        (p0, p1)[s // 2][:, :, pl.ds((s % 2) * seg, seg)] = part.reshape(NY, 16, seg)
-
-    pp, sm, rm = (p0, p1), (sm0, sm1), (rm0, rm1)
-    m_steps = {(d, s): (NY // 2 if d == s else NY // 2 - 1) for d in range(2) for s in range(2)}
+        pp[s][:, :, pl.ds(0, seg)] = mm(both, guv[c * 4 + s], 1, 1).reshape(NY, 16, seg)
+
+    arrived(w2.at[other, y], bs_r.at[NY])
+    for d in range(2):
+        for t in range(NY // 2 - d):
+            arrived(w2.at[other, whose(d, t)], bs_r.at[d * (NY // 2) + t])
+    keeps = []
+
+    def o_place(zz, p):
+        low = (zz // per_half) * (4 * seg) + (14 * (zz % per_half)) // 3 * 128 + p * 128
+        return dg.at[:, pl.ds(pl.multiple_of(low, 128), 128)]
+
+    def o_when(zz, p, f):
+        if p < TILES - 1:
+            f()
+        else:
+            pl.when(zz % 3 != 0)(f)
+
+    def o_long(d, p):
+        return NZ // 2 - (d != p % 2)
+
+    def o_keep(zz, p, k):
+        copy = pltpu.make_async_copy(ov.at[zz, p], o_place(zz, p), loc.at[k])
+        o_when(zz, p, copy.start)
+        keeps.append((copy, zz, p))
+
+    def o_send(d, p, t):
+        g = 1 if d == 0 else -1
+        zz = (z - g * t + NZ) % NZ
+        k = d * (NZ // 2) + t
+        ref = ov.at[zz, p]
+        copy = pltpu.make_async_remote_copy(
+            src_ref=ref, dst_ref=ref, send_sem=o_s.at[p, k], recv_sem=o_r.at[p, k],
+            device_id=at((z + g + NZ) % NZ, x, y, c), device_id_type=MESH,
+        )
+        o_when(zz, p, copy.start)
+        sent.append((copy, zz, p))
+
+    def o_turn(t):
+        for p in range(TILES):
+            for d in range(2):
+                if t < o_long(d, p):
+                    g = 1 if d == 0 else -1
+                    zz = (z - g * (t + 1) + NZ) % NZ
+                    k = d * (NZ // 2) + t
+                    o_when(zz, p, lambda: arrived(ov.at[zz, p], o_r.at[p, k]))
+                    if t + 1 < o_long(d, p):
+                        o_send(d, p, t + 1)
+                    o_keep(zz, p, p * (NZ + 1) + k)
+
+    sent = []
+    mine = mm(hv[...].reshape(-1, 128), w2[...].reshape(-1, SPAN), 0, 0).astype(bf16)
+    for p in range(TILES):
+        ov[z, p] = mine[:, p * 128:p * 128 + 128]
+        o_send(0, p, 0)
+        o_send(1, p, 0)
+        o_keep(z, p, p * (NZ + 1) + NZ)
+
+    m_steps = {(d, s): (NY // 2 if d == s % 2 else NY // 2 - 1) for d in range(2) for s in range(4)}
 
     def m_number(d, t):
         return d * (NY // 2) + t
@@ -358,44 +406,39 @@
 
     for s in range(4):
         arrived(qr.at[s], q_r.at[s])
-        ref = (p0, p1)[s // 2]
-        cols = pl.ds((s % 2) * seg, seg)
-        ref[:, :, cols] = ref[:, :, cols] + qr[s].astype(f32).reshape(NY, 16, seg)
-        if s % 2:
-            m_send(0, s // 2, 0)
-            m_send(1, s // 2, 0)
+        ref = pp[s]
+        ref[:, :, pl.ds(0, seg)] = ref[:, :, pl.ds(0, seg)] + qr[s].astype(f32).reshape(NY, 16, seg)
+        m_send(0, s, 0)
+        m_send(1, s, 0)
     for t in range(NY // 2):
-        for s in range(2):
+        o_turn(t)
+        for s in range(4):
             for d in range(2):
                 if t < m_steps[d, s]:
                     n = m_number(d, t)
                     arrived(rm[s].at[n], m_r.at[s * 8 + n])
                     if t + 1 < m_steps[d, s]:
                         m_send(d, s, t + 1)
-        o_turn(t)
 
     i64 = iota((64, 16), 0)
     k64 = iota((64, 16), 1)
-    totals = []
-    for s in range(2):
+    out = jnp.zeros((64, seg), f32)
+    source = (i64 // 8) * CAP + i64 % CAP
+    for s in range(4):
         total = pp[s][y]
         for d in range(2):
             total = total + rm[s][m_number(d, m_steps[d, s] - 1)].astype(f32)
-        totals.append(total)
-    out = jnp.zeros((64, seg), f32)
-    source = (i64 // 8) * CAP + i64 % CAP
-    for s in range(4):
         pick = one_hot((source == k64) & ((i64 // CAP) % 4 == s))
-        for piece in split(totals[s // 2][:, (s % 2) * seg:(s % 2) * seg + seg]):
+        for piece in split(total[:, 0:seg]):
             out = out + mm(pick, piece)
     products = jnp.zeros((64, 128), f32)
     pick = one_hot((source == k64) & ((i64 // CAP) % 4 == 0))
-    for piece in split(totals[1][:, subw:subw + 128]):
+    for piece in split(total[:, seg:seg + 128]):
         products = products + mm(pick, piece)
     ys[:, :, :, pl.ds(0, seg)] = out.reshape(NX, 2, 8, seg)
     ys[:, :, :, pl.ds(seg, 128)] = products.reshape(NX, 2, 8, 128)
     keep = pltpu.make_async_copy(ys.at[x, c], yr.at[x, c], y_r.at[x * 2 + c])
-    for dx in range(NX):
+    for dx in (2, 1, 3, 0):
         for dc in range(2):
             if dx == 0 and dc == 0:
                 keep.start()
@@ -407,7 +450,10 @@
     for xx in range(NX):
         for cc in range(2):
             arrived(yr.at[xx, cc], y_r.at[xx * 2 + cc])
-    keep_out.wait()
+    for copy, zz, p in keeps:
+        o_when(zz, p, copy.wait)
+    for copy, zz, p in sent:
+        o_when(zz, p, copy.wait_send)
     for item in pending:
         if isinstance(item, tuple):
             copy, cond = item
@@ -420,24 +466,12 @@
 
 
 def final_kernel(
-    logits_ref, group_ref, member_ref, yr_ref, dg, token_out, logit_ref, down_out, stage, sems
+    logits_ref, group_ref, member_ref, yr_ref, dg, token_out, logit_ref, down_out, stage, whole, sems
 ):
     seg = stage.shape[2]
-    per_half = NZ // 2
     copies = []
-    for zz in range(NZ):
-        k = zz % per_half
-        start = (14 * k) // 3
-        width = ((14 * (k + 1)) // 3 - start) * 128
-        start = (zz // per_half) * 4 * seg + start * 128
-        for s in range(2):
-            copy = pltpu.make_async_copy(
-                dg.at[zz, s, :, pl.ds(0, width)],
-                down_out.at[pl.ds(s * 64, 64), pl.ds(start, width)],
-                sems.at[8 + zz * 2 + s],
-            )
-            copy.start()
-            copies.append(copy)
+    fetch = pltpu.make_async_copy(dg, whole, sems.at[8])
+    fetch.start()
     affinity, affinity_sum, hits, slot8, gate8 = routing(logits_ref[...], group_ref[...], member_ref[...])
     grads = yr_ref[:, :, :, 0:seg].reshape(64, seg)
     pieces = jnp.concatenate(split(grads), axis=0)
@@ -450,6 +484,10 @@
         copy = pltpu.make_async_copy(stage.at[j], token_out.at[:, pl.ds(j * seg, seg)], sems.at[j])
         copy.start()
         copies.append(copy)
+    fetch.wait()
+    copy = pltpu.make_async_copy(whole, down_out, sems.at[9])
+    copy.start()
+    copies.append(copy)
     products = yr_ref[:, :, :, seg:seg + 128].reshape(64, 128)
     folded = jnp.zeros((8, 128), f32)
     for piece in split(products):
@@ -483,37 +521,36 @@
         pltpu.VMEM((NX, 2, 8, seg), f32),
         pltpu.VMEM((NX, 2, 8, seg), f32),
         pltpu.VMEM((2, 2, NY, 16, subw), bf16),
-        pltpu.VMEM((2, 2, NY, 3, 16, SPAN), bf16),
-        pltpu.VMEM((2, 2, NY, 3, 16, 128), bf16),
+        pltpu.VMEM((2, NY, NZ // 2, 16, SPAN), bf16),
+        pltpu.VMEM((2, NY, NZ // 2, 16, 128), bf16),
         pltpu.VMEM((128, 128), f32),
         pltpu.VMEM((128, 128), f32),
-        pltpu.VMEM((2, 64, SPAN), bf16),
+        pltpu.VMEM((NZ, TILES, 128, 128), bf16),
         pltpu.VMEM((4, 128, seg), bf16),
         pltpu.VMEM((4, 128, seg), bf16),
-        pltpu.VMEM((NY, 16, subw), f32),
-        pltpu.VMEM((NY, 16, subw + 128), f32),
-        pltpu.VMEM((8, 16, subw), bf16),
-        pltpu.VMEM((8, 16, subw + 128), bf16),
-        pltpu.VMEM((8, 16, subw), bf16),
-        pltpu.VMEM((8, 16, subw + 128), bf16),
+    ]
+    widths = (seg, seg, seg, seg + 128)
+    scratch += [pltpu.VMEM((NY, 16, w), f32) for w in widths]
+    scratch += [pltpu.VMEM((8, 16, w), bf16) for w in widths * 2]
+    scratch += [
         pltpu.VMEM((NX, 2, 8, seg + 128), f32),
         dma((28,)),
         dma((8,)), dma((8,)),
         dma((6,)), dma((6,)),
-        dma((16,)), dma((16,)), dma((18,)), dma((18,)),
-        dma((16,)), dma((16,)), dma((18,)), dma((18,)),
+        dma((2, 8)), dma((2, 8)), dma((2, 9)), dma((2, 9)),
+        dma((6, 8)), dma((6, 8)), dma((9,)), dma((9,)),
         dma((12,)), dma((12,)),
-        dma((24,)), dma((24,)),
+        dma((TILES, 12)), dma((TILES, 12)),
         dma((4,)), dma((4,)),
-        dma((16,)), dma((16,)),
+        dma((32,)), dma((32,)),
         dma((8,)), dma((8,)),
-        dma((1,)),
+        dma((TILES * (NZ + 1),)),
     ]
     yr, dg = pl.pallas_call(
         main_kernel,
         out_shape=(
             jax.ShapeDtypeStruct((NX, 2, 8, seg + 128), f32),
-            jax.ShapeDtypeStruct((NZ, 2, 64, SPAN), bf16),
+            jax.ShapeDtypeStruct((128, width), bf16),
         ),
         in_specs=[vmem] * 5 + [hbm] * 4,
         out_specs=(hbm, hbm),
@@ -531,7 +568,11 @@
         ),
         in_specs=[vmem] * 4 + [hbm],
         out_specs=(hbm, vmem, hbm),
-        scratch_shapes=[pltpu.VMEM((8, tokens, seg), bf16), dma((32,))],
+        scratch_shapes=[
+            pltpu.VMEM((8, tokens, seg), bf16),
+            pltpu.VMEM((128, width), bf16),
+            dma((10,)),
+        ],
         compiler_params=pltpu.CompilerParams(vmem_limit_bytes=62 * 1024 * 1024),
     )(logits_t, group_t, member_t, yr, dg)
     return token_grad, logit_grad.T, down_grad

time: 152 us -> 84.5 us (0.56)
  the two profiles are of different devices: /device:TPU:6 before, /device:TPU:1 now
where the time goes in v3:
time: 84.5 us; the launch traced here: 84.2 us
  Pallas kernels  83.6 us (99%)
    pallas_call x1, Pallas kernels, body(): pl.pallas_call(main_kernel, out_shape=(jax.ShapeDtypeStruct((NX, 2, 8, se...  79.1 us
    pallas_call x1, Pallas kernels, body(): pl.pallas_call(final_kernel, out_shape=(jax.ShapeDtypeStruct((tokens, wid...  4.41 us

profile of v3, /device:TPU:1, one launch (start us, length us, event | category | flops | bytes accessed | tf_op | source)
XLA Modules:
  0.0 84.2 jit_solution(17824975617728422951)
XLA Ops:
  0.6 79.1 %shard_map.112 = (f32[4,2,8,1024]{3,2,1,0:T(8,128)}, bf16[128,7168]{1,0:T(8,128)(2,1)}) custom-call(f32[8,128]{1,0:T(8,128)} %bitcast.4, s32[8,128]{1,0:T(8,128)} %bitcast.6, s32[8,128]{1,0:T(8,128)} %bitcast.8, bf16[128,128]{1,0:T(8,128)(2,1)} %sg_ref.1, bf16[128,128]{1,0:T(8,128)(2,1)} %su_ref.1, bf16[128,7168]{1,0:T(8,128)(2,1)} %cot_hbm.1, ...), custom_call_target="tpu_custom_call" | custom-call | tf_op jit(solution)/shard_map/pallas_call | solution.py:549
  79.8 4.4 %shard_map.113 = (bf16[128,7168]{1,0:T(8,128)(2,1)}, f32[8,128]{1,0:T(8,128)}, bf16[128,7168]{1,0:T(8,128)(2,1)}) custom-call(f32[8,128]{1,0:T(8,128)} %bitcast.5, s32[8,128]{1,0:T(8,128)} %bitcast.7, s32[8,128]{1,0:T(8,128)} %bitcast.9, f32[4,2,8,1024]{3,2,1,0:T(8,128)} %get-tuple-element.8.yr_ref, bf16[128,7168]{1,0:T(8,128)(2,1)} %get-tuple-element.9.dg), custom_call_target="tpu_custom_call" | custom-call | tf_op jit(solution)/shard_map/pallas_call | solution.py:562
